TPU v7x, 512 devices: a whole 4x4x16 slice. The times are simulated.
512 devices in a mesh: shot: 64 (over x, z_hi, y, core), tm: 8 (over z_lo).
Axes of the slice: x: 4, y: 4, z: 16 (z_hi: 2, z_lo: 8; z = z_hi * 8 + z_lo), core: 2. Of those that a mesh axis runs over, the one named last changes fastest.
Arguments:
- shot_window: bfloat16 [768, 32, 256], P('shot'), may hold values from -0.125 to 0.125
- receiver_data: bfloat16 [512, 192, 256], P('tm', 'shot'), may hold values from -6 to 6
- apertures: int32 [768, 4], P('shot'), may hold values from 0 to 7
- taper_index: int32 [768, 4], P('shot'), may hold values from 0 to 15
- taper_table: float32 [16], replicated, may hold values from 0.2 to 1
Outputs:
- multiples: bfloat16 [512, 768, 192], P('tm', 'shot')
All inputs are finite; a program needn't handle non-finite values.
Results may differ from a plain program's by a relative error of at most 0.012.
Values may be sent and summed in bfloat16 or wider, within the bound.
A program may use at most 128 MiB of HBM per device.

v0:
```python
import jax
import jax.numpy as jnp
from jax import lax
from jax.sharding import PartitionSpec as P

NKB = 8


def from_behind(value, axis, steps):
    count = lax.axis_size(axis)
    first, last = (max(0, -steps), min(count, count - steps))
    return lax.ppermute(value, axis, [(source, source + steps) for source in range(first, last)])


def tapered_operator(shot_window, apertures, taper_index, taper_table, nblocks):
    table_size = taper_table.shape[0]
    picked = jnp.sum(
        jnp.where(
            taper_index[:, :, None] == jnp.arange(table_size, dtype=jnp.int32)[None, None, :],
            taper_table[None, None, :],
            jnp.float32(0.0),
        ),
        axis=2,
    )
    weight = jnp.sum(
        jnp.where(
            apertures[:, :, None] == jnp.arange(nblocks, dtype=jnp.int32)[None, None, :],
            picked[:, :, None],
            jnp.float32(0.0),
        ),
        axis=1,
    )
    block_size = shot_window.shape[2] // nblocks
    spread = jnp.repeat(weight, block_size, axis=1)
    return (shot_window.astype(jnp.float32) * spread[:, None, :]).astype(jnp.bfloat16)


def toeplitz_operator(operator):
    lag_count = operator.shape[1]
    out_pos = jnp.arange(lag_count, dtype=jnp.int32)
    in_pos = jnp.arange(2 * lag_count, dtype=jnp.int32)
    lag_index = lag_count + out_pos[:, None] - in_pos[None, :]
    valid = (lag_index >= 0) & (lag_index < lag_count)
    clipped = jnp.clip(lag_index, 0, lag_count - 1)
    spread = operator[:, clipped, :]
    return jnp.where(valid[None, :, :, None], spread, jnp.zeros_like(spread))


def convolve_blocks(banded, extended):
    lag_count = banded.shape[1]
    nwindows = (extended.shape[0] - lag_count) // lag_count
    windows = jnp.stack(
        [
            lax.slice_in_dim(extended, b * lag_count, b * lag_count + 2 * lag_count, axis=0)
            for b in range(nwindows)
        ]
    )
    result = jnp.einsum("sjck,bcnk->bjsn", banded, windows, preferred_element_type=jnp.float32)
    return result.reshape(nwindows * lag_count, result.shape[2], result.shape[3])


def body(shot_window, receiver_data, apertures, taper_index, taper_table):
    nblocks = NKB
    operator = tapered_operator(shot_window, apertures, taper_index, taper_table, nblocks)
    lag_count = operator.shape[1]
    banded = toeplitz_operator(operator)
    slab = receiver_data.shape[0]
    extended = jnp.pad(
        lax.all_gather(receiver_data, "shot", axis=1, tiled=True),
        ((lag_count, lag_count), (0, 0), (0, 0)),
    )
    full_span = convolve_blocks(banded, extended)
    leading = full_span[:slab]
    carried = from_behind(full_span[slab:].astype(jnp.bfloat16), "tm", 1).astype(jnp.float32)
    total = leading.at[:lag_count].add(carried)
    return total.astype(jnp.bfloat16)


def solution(mesh):
    in_specs = (P("shot", None, None), P("tm", "shot", None), P("shot", None), P("shot", None), P())
    out_specs = P("tm", "shot", None)
    return jax.shard_map(body, mesh=mesh, in_specs=in_specs, out_specs=out_specs, check_vma=False)
```

profile of v0, /device:TPU:1, one launch (start us, length us, event | category | flops | bytes accessed | tf_op | source)
XLA Modules:
  0.0 210.0 jit_solution(13967082633814393315)
XLA Ops:
  6.5 0.0 all-gather.2.cloned.1.call-start
  6.5 0.7 all-gather.2.cloned.1.call-update
  7.3 0.8 copy.26
  8.0 0.8 select_reduce_fusion
  8.8 0.1 copy.27
  8.9 0.7 select_reduce_fusion.1
  9.6 0.1 copy.28
  9.7 0.1 compare_select_fusion
  9.8 0.1 reshape.119
  9.9 0.1 broadcast_in_dim.53
  9.9 0.1 mul.10
  10.0 1.0 multiply_convert_fusion
  11.1 18.9 %gather_fusion = bf16[2048,12,256]{2,1,0:T(8,128)(2,1)} fusion(bf16[12,32,256]{2,0,1:T(8,128)(2,1)S(1)} %multiply_convert_fusion, s32[2048]{0:T(1024)S(1)} %broadcast_clamp_fusion), kind=kCustom, calls=%fused_computation | custom fusion | bytes 25174016 | tf_op jit(solution)/shard_map/gather | solution.py:45
  30.0 136.7 %all-gather.2.cloned.1.call-done = bf16[64,192,256]{2,0,1:T(8,128)(2,1)} async-done(((bf16[64,3,256]{2,0,1:T(8,128)(2,1)}), bf16[64,192,256]{2,0,1:T(8,128)(2,1)}) %all-gather.2.cloned.1.call-update) | async-done | bytes 6291472 | tf_op jit(solution)/shard_map/all_gather | solution.py:69
  166.7 6.3 %copy.42 = bf16[64,192,256]{2,1,0:T(8,128)(2,1)S(1)} copy(bf16[64,192,256]{2,0,1:T(8,128)(2,1)} %all-gather.2.cloned.1.call-done) | data formatting | bytes 12582912 | tf_op jit(solution)/shard_map/all_gather | solution.py:69
  173.0 1.5 fusion.7
  174.6 22.1 %fusion.10 = f32[3,32,12,192]{3,1,2,0:T(8,128)S(1)} fusion(bf16[32,64,12,256]{3,2,1,0:T(8,128)(2,1)} %bitcast.39, pred[32,64]{0,1:T(8,128)(4,1)S(1)} %fusion.18, bf16[1,64,192,256]{3,2,1,0:T(8,128)(2,1)S(1)} %get-tuple-element.18, bf16[1,64,192,256]{3,2,1,0:T(8,128)(2,1)S(1)} %bitcast.38, bf16[1,64,192,256]{3,2,1,0:T(8,128)(2,1)S(1)} %get-tuple-element.17), kind=kOutput, calls=%fused_computation.15 | convolution fusion | flops 7310671872 | bytes 32344064 | tf_op jit(solution)/shard_map/sjck,bcnk->bjsn/dot_general | solution.py:58
  196.7 1.3 collective-permute-start
  198.0 0.1 slice.52
  198.1 0.8 copy.30
  198.9 3.5 %collective-permute-done = bf16[32,12,192]{2,0,1:T(8,128)(2,1)S(1)} collective-permute-done((bf16[32,12,192]{2,0,1:T(8,128)(2,1)S(1)}, bf16[32,12,192]{2,0,1:T(8,128)(2,1)S(1)}, u32[]{:S(2)}, u32[]{:S(2)}) %collective-permute-start) | collective-permute-done | bytes 147488 | tf_op jit(solution)/shard_map/ppermute | solution.py:12
  202.4 0.7 fusion.14
  (4 shorter events, 0.0 us)
Async XLA Ops:
  6.5 160.1 %all-gather.2.cloned.1.call-start = ((), (), s32[]{:S(2)}) async-start(), calls=%async_computation | async-start | bytes 6389760 | tf_op jit(solution)/shard_map/all_gather | solution.py:69
  196.7 5.7 %collective-permute-start = (bf16[32,12,192]{2,0,1:T(8,128)(2,1)S(1)}, bf16[32,12,192]{2,0,1:T(8,128)(2,1)S(1)}, u32[]{:S(2)}, u32[]{:S(2)}) collective-permute-start(bf16[32,12,192]{2,0,1:T(8,128)(2,1)S(1)} %fusion.15), channel_id=1, source_target_pairs={{0,1},{1,2},{2,3},{3,4},{4,5},{5,6},{6,7},{8,9},{9,10},{10,11},{11... | collective-permute-start | bytes 442376 | tf_op jit(solution)/shard_map/ppermute | solution.py:12
Sparse Core Ops, SparseCore 0:
  11.9 154.7 all-gather.1
where the time goes:
time: 212 us; the launch traced here: 210 us
  waiting for transfers between devices  141 us (67%)
  local copies, waits for them, and re-layouts  28.8 us (14%)
  matrix products  22.1 us (10%)
  between operations  13.5 us (6%)
  other arithmetic  3.39 us (2%)
    all_gather x1, waiting for transfers between devices, body(): lax.all_gather(receiver_data, 'shot', axis=1, tiled=True)  137 us
    dot_general x1, matrix products, convolve_blocks(): jnp.einsum('sjck,bcnk->bjsn', banded, windows, preferred_element_type=jnp...  22.1 us
    gather x1, local copies, waits for them, and re-layouts, toeplitz_operator(): spread = operator[:, clipped, :]  18.9 us
    all_gather x1, local copies, waits for them, and re-layouts, body(): lax.all_gather(receiver_data, 'shot', axis=1, tiled=True)  6.35 us
  transfers between devices with their start and end apart: 2, of which 2 were waited for; matrix products, arithmetic and copies ran while one was open for 11% of the time, Pallas kernels for 0%

commit v1 on v0

v1 whole, which is shorter than its diff:
```python
import jax
import jax.numpy as jnp
from jax import lax
from jax.experimental import pallas as pl
from jax.experimental.pallas import tpu as pltpu
from jax.sharding import PartitionSpec as P

MESH = pl.DeviceIdType.MESH
NX, NY, NH, NC, NTM = 4, 4, 2, 2, 8
NZ = NH * NTM
NKB, LAG, K = 8, 32, 256
SH, RC, TS = 12, 3, 64
S2 = 2 * SH
UR = NY * RC
NCH = 3
R = 192
HEAD, ROWS, WIN = 16, 112, 96
ORDER = (0, 1, 3, 2)
HR = 80
NSEM = 80

HALF = ((0, 32), (32, 32))
PLUS = ((16, 16), (32, 16))
MINUS = ((0, 16), (48, 16))


def device(x, y, h, c, t):
    return (((x * NH + h) * NY + y) * NC + c, t)


def kernel(x_ref, shot_hbm, aper_ref, tidx_ref, table_ref, out_ref,
           xg, rz, shot_ref, op_own, op_sib, op_f32, op_all, wt, prod, main, half_f32, halo_out, halo_in,
           ex_out, ex_in, wide, send_sem, recv_sem, z_send, z_recv, op_sem, halo_sem, ex_sem, local_sem):
    shot_i = lax.axis_index("shot")
    t = lax.axis_index("tm")
    c = shot_i % 2
    y = (shot_i // 2) % 4
    h = (shot_i // 8) % 2
    x = shot_i // 16
    z = h * NTM + t
    xs = [(x + d) % NX for d in range(NX)]
    ys = [RC * ((y + d) % NY) for d in range(NY)]
    zp = (z + 4) % NZ
    zm = (z + NZ - 4) % NZ
    up = device(x, y, zp // NTM, c, zp % NTM)
    down = device(x, y, zm // NTM, c, zm % NTM)
    sibling = device(x, y, h, 1 - c, t)
    after = device(x, y, h, c, (t + 1) % NTM)
    before = device(x, y, h, c, (t + NTM - 1) % NTM)
    near = {
        ("x", 1): device((x + 1) % NX, y, h, c, t),
        ("x", -1): device((x + NX - 1) % NX, y, h, c, t),
        ("y", 1): device(x, (y + 1) % NY, h, c, t),
        ("y", -1): device(x, (y + NY - 1) % NY, h, c, t),
    }
    partners = list(near.values()) + [up, down, sibling, after, before]

    own_copy = pltpu.make_async_copy(x_ref, xg.at[0, x, pl.ds(ys[0], RC), pl.ds(HEAD, TS)], local_sem.at[0])
    own_copy.start()
    shot_copy = pltpu.make_async_copy(shot_hbm, shot_ref, local_sem.at[1])
    shot_copy.start()

    for l in range(2):
        xg[l, :, :, 0:HEAD, :] = jnp.zeros((NX, UR, HEAD, K), jnp.bfloat16)
        xg[l, :, :, HEAD + TS:ROWS, :] = jnp.zeros((NX, UR, ROWS - HEAD - TS, K), jnp.bfloat16)
    half_f32[...] = jnp.zeros_like(half_f32)

    barrier = pltpu.get_barrier_semaphore()
    for who in partners:
        pl.semaphore_signal(barrier, inc=1, device_id=who, device_id_type=MESH)
    pl.semaphore_wait(barrier, len(partners))

    sends = []
    kinds = {}

    def slot(l, dx, dy, rows):
        return xg.at[l, xs[dx % NX], pl.ds(ys[dy % NY], RC), pl.ds(HEAD + rows[0], rows[1])]

    def remote(src, dst, ssem, rsem, who):
        return pltpu.make_async_remote_copy(src_ref=src, dst_ref=dst, send_sem=ssem, recv_sem=rsem,
                                            device_id=who, device_id_type=MESH)

    def start(copy):
        copy.start()
        sends.append(copy)
        return copy

    z_first = [start(remote(x_ref.at[:, pl.ds(32 * d, 32)], rz.at[d], z_send.at[d], z_recv.at[d], who))
               for d, who in ((0, up), (1, down))]

    def send(l, n, oa, ob, rows, axis, way):
        first = "y" if n == 0 else "x"
        dx, dy = (ob, oa) if first == "y" else (oa, ob)
        step = way if axis == first else 0
        other = way if axis != first else 0
        key = (l, n, oa - step, ob - other, rows)
        k = kinds.setdefault(("sem",) + key + (axis, way), len([q for q in kinds if q[0] == "sem"]))
        ref = slot(l, dx, dy, rows)
        src = ref
        if l == 0 and oa == 0 and ob == 0:
            src = x_ref.at[:, pl.ds(rows[0], rows[1])]
        kinds[key] = start(remote(src, ref, send_sem.at[k], recv_sem.at[k], near[(axis, way)]))

    def recv(l, n, oa, ob, rows):
        kinds[(l, n, oa, ob, rows)].wait_recv()

    def axes(n):
        return ("y", "x") if n == 0 else ("x", "y")

    def base(l, n):
        a, b = axes(n)
        for axis in (a, b):
            for way in (1, -1):
                send(l, n, 0, 0, HALF[n], axis, way)

    def round1(l):
        for n in (0, 1):
            a, b = axes(n)
            for off, way, piece in ((-1, 1, PLUS), (1, -1, MINUS)):
                recv(l, n, off, 0, HALF[n])
                send(l, n, off, 0, piece[n], a, way)
                for w in (1, -1):
                    send(l, n, off, 0, HALF[n], b, w)
        for n in (0, 1):
            a, b = axes(n)
            for off, way, piece in ((-1, 1, PLUS), (1, -1, MINUS)):
                recv(l, n, 0, off, HALF[n])
                send(l, n, 0, off, piece[n], b, way)

    def round2(l):
        for n in (0, 1):
            a, b = axes(n)
            recv(l, n, -2, 0, PLUS[n])
            recv(l, n, 2, 0, MINUS[n])
            for w in (1, -1):
                send(l, n, 2, 0, HALF[n], b, w)
        for oa in (-1, 1):
            for n in (0, 1):
                a, b = axes(n)
                for off, way, piece in ((-1, 1, PLUS), (1, -1, MINUS)):
                    recv(l, n, oa, off, HALF[n])
                    send(l, n, oa, off, piece[n], b, way)
        for n in (0, 1):
            recv(l, n, 0, -2, PLUS[n])
            recv(l, n, 0, 2, MINUS[n])

    def round3(l):
        for n in (0, 1):
            a, b = axes(n)
            for off, way, piece in ((-1, 1, PLUS), (1, -1, MINUS)):
                recv(l, n, 2, off, HALF[n])
                send(l, n, 2, off, piece[n], b, way)

    def round4(l):
        for oa in (-1, 1, 2):
            for n in (0, 1):
                recv(l, n, oa, -2, PLUS[n])
                recv(l, n, oa, 2, MINUS[n])

    base(0, 0)
    base(0, 1)

    wt[...] = jnp.zeros_like(wt)
    tidx = tidx_ref[...]
    aper = aper_ref[...]
    picked = jnp.zeros(tidx.shape, jnp.float32)
    for j in range(16):
        picked = picked + jnp.where(tidx == j, table_ref[j], jnp.float32(0.0))
    for b in range(NKB):
        wt[b:b + 1, 0:SH] = jnp.sum(jnp.where(aper == b, picked, jnp.float32(0.0)), axis=0, keepdims=True)
    weight = wt[...].T
    block = lax.broadcasted_iota(jnp.int32, (16, K), 1) // (K // NKB)
    spread = jnp.zeros((16, K), jnp.float32)
    for b in range(NKB):
        spread = jnp.where(block == b, weight[0:16, b:b + 1], spread)
    shot_copy.wait()
    for s in range(SH):
        op_own[s] = (shot_ref[s].astype(jnp.float32) * spread[s:s + 1, :]).astype(jnp.bfloat16)
    op_copy = start(remote(op_own, op_sib, op_sem.at[0], op_sem.at[1], sibling))

    round1(0)
    z_second = []
    for d, who in ((0, up), (1, down)):
        z_first[d].wait_recv()
        z_second.append(start(remote(rz.at[d], slot(1, 0, 0, HALF[d]), z_send.at[2 + d], z_recv.at[2 + d], who)))

    def place(ref, s, row):
        v = ref[s].astype(jnp.float32)
        for q in range(2):
            op_f32[q, pl.ds(row, LAG, stride=S2), :] = v[:, q * 128:(q + 1) * 128]

    for s in range(SH):
        place(op_own, s, s if s < 8 else 8 + s)
    op_copy.wait_recv()
    for s in range(SH):
        place(op_sib, s, 8 + s if s < 8 else 12 + s)
    for q in range(2):
        for a in range(2):
            cols = a * K + q * 128
            op_all[:, cols:cols + 128] = op_f32[q, a * LAG * SH:(a + 1) * LAG * SH, :].astype(jnp.bfloat16)

    lane = lax.broadcasted_iota(jnp.int32, (S2, 128), 1)

    def compute(g):
        l, ux = g // 4, xs[ORDER[g % 4]]
        for r0, nr in ((0, 8), (8, 4)):
            late = xg[l, ux, r0:r0 + nr, HEAD:HEAD + WIN, :].reshape(nr * WIN, K)
            early = xg[l, ux, r0:r0 + nr, 0:WIN, :].reshape(nr * WIN, K)
            prod[:, r0 * WIN:(r0 + nr) * WIN] = lax.dot_general(
                op_all[...], jnp.concatenate([late, early], axis=1), (((1,), (1,)), ((), ())),
                preferred_element_type=jnp.float32)
        for j in range(NCH):
            acc = prod[0:S2, j * 4 * WIN:(j + 1) * 4 * WIN]
            for b in range(1, LAG // 2):
                acc = acc + pltpu.roll(prod[b * S2:(b + 1) * S2, j * 4 * WIN:(j + 1) * 4 * WIN], b, 1)
            v0, v1, v2 = acc[:, 0:128], acc[:, 128:256], acc[:, 256:384]
            index = g * NCH + j
            main[2 * index] = jnp.where(lane < 64, v0, pltpu.roll(jnp.where(lane >= 96, v0, v1), 96, 1))
            main[2 * index + 1] = jnp.where(lane < 64, pltpu.roll(v2, 96, 1), v1)
            halo = jnp.where(lane < 32, v2, jnp.where(lane < 64, v1, jnp.where(lane < 96, v0, v2)))
            half_f32[g * HR + j * S2:g * HR + (j + 1) * S2, :] = halo

    def halo_copy(g):
        return remote(halo_out.at[g], halo_in.at[g], halo_sem.at[g], halo_sem.at[8 + g], after)

    def send_halo(g):
        halo_out[g] = half_f32[g * HR:(g + 1) * HR, :].astype(jnp.bfloat16)

        @pl.when(t < NTM - 1)
        def _():
            halo_copy(g).start()

    lane8 = lax.broadcasted_iota(jnp.int32, (8, 128), 1)

    rows_of = [xs[d] * 48 for d in ORDER]

    def widen(g, j, q, first8, second8, base_s, core):
        for k in range(2):
            ry = 4 * j + ((0, 1), (3, 2))[q][k]
            row = rows_of[g % 4] + 24 * ((h + g // 4) % 2) + core * 3 + (ry // 3) * 6 + ry % 3
            mask = (lane8 < 64) if k == 0 else (lane8 >= 64)
            wide[pl.ds(base_s * R + row, 8, stride=R), :] = jnp.where(mask, second8, 0.0)
            wide[pl.ds(row, 8, stride=R), :] = jnp.where(mask, first8, 0.0)

    def exchange_copy(g):
        rows = pl.ds(g * 2 * NCH, 2 * NCH)
        return remote(ex_out.at[rows], ex_in.at[rows], ex_sem.at[g], ex_sem.at[8 + g], sibling)

    copies = {}

    def finish(g):
        @pl.when(t > 0)
        def _():
            halo_copy(g).wait_recv()
            half_f32[g * HR:(g + 1) * HR, :] = halo_in[g].astype(jnp.float32)

        @pl.when(t == 0)
        def _():
            half_f32[g * HR:(g + 1) * HR, :] = jnp.zeros((HR, 128), jnp.float32)

        for j in range(NCH):
            packed = half_f32[g * HR + j * S2:g * HR + (j + 1) * S2, :]
            by32, by64 = pltpu.roll(packed, 32, 1), pltpu.roll(packed, 64, 1)
            for q in range(2):
                index = 2 * (g * NCH + j) + q
                part = jnp.where(lane < 64, by64, by32) if q == 0 else jnp.where(lane < 64, by32, by64)
                v = main[index] + jnp.where(lane % 64 < 32, part, 0.0)
                v = v.astype(jnp.bfloat16).astype(jnp.float32)
                ex_out[index] = v[8:24].astype(jnp.bfloat16)
                widen(g, j, q, v[0:8], v[16:24], 8, c)
        copies[g] = start(exchange_copy(g))

    def accept(g):
        copies[g].wait_recv()
        for j in range(NCH):
            for q in range(2):
                v = ex_in[2 * (g * NCH + j) + q].astype(jnp.float32)
                widen(g, j, q, v[0:8], v[8:16], 4, 1 - c)

    def unit(g):
        compute(g)
        send_halo(g)

    round2(0)
    own_copy.wait()
    unit(0)
    round3(0)
    for n in (0, 1):
        z_second[n].wait_recv()
        base(1, n)
    round4(0)
    unit(1)
    unit(2)
    round1(1)
    unit(3)
    finish(0)
    finish(1)
    round2(1)
    unit(4)
    finish(2)
    round3(1)
    finish(3)
    accept(0)
    accept(1)
    round4(1)
    unit(5)
    unit(6)
    unit(7)
    accept(2)
    accept(3)
    for g in (4, 5, 6, 7):
        finish(g)
    for g in (4, 5, 6, 7):
        accept(g)

    both = lax.broadcasted_iota(jnp.int32, (TS, 128), 1) % TS == lax.broadcasted_iota(jnp.int32, (TS, 128), 0)
    both = jnp.where(both, 1.0, 0.0).astype(jnp.bfloat16)

    def turn(s, carry):
        block = wide[pl.ds(pl.multiple_of(s * R, 8), R), :].astype(jnp.bfloat16)
        out_ref[s] = lax.dot_general(both, block, (((1,), (1,)), ((), ())),
                                     preferred_element_type=jnp.float32).astype(jnp.bfloat16)
        return carry

    lax.fori_loop(0, SH, turn, 0)

    for copy in sends:
        copy.wait_send()

    @pl.when(t < NTM - 1)
    def _():
        for g in range(8):
            halo_copy(g).wait_send()


def body(shot_window, receiver_data, apertures, taper_index, taper_table):
    gathered = jnp.transpose(receiver_data, (1, 0, 2))
    vmem = pl.BlockSpec(memory_space=pltpu.VMEM)
    bf, f4 = jnp.bfloat16, jnp.float32
    dma = pltpu.SemaphoreType.DMA
    out = pl.pallas_call(
        kernel,
        out_shape=jax.ShapeDtypeStruct((SH, TS, R), bf),
        in_specs=[pl.BlockSpec(memory_space=pl.ANY), pl.BlockSpec(memory_space=pl.ANY), vmem, vmem, pl.BlockSpec(memory_space=pltpu.SMEM)],
        out_specs=vmem,
        scratch_shapes=[
            pltpu.VMEM((2, NX, UR, ROWS, K), bf),
            pltpu.VMEM((2, RC, 32, K), bf),
            pltpu.VMEM((SH, LAG, K), bf),
            pltpu.VMEM((SH, LAG, K), bf),
            pltpu.VMEM((SH, LAG, K), bf),
            pltpu.VMEM((2, LAG * S2, 128), f4),
            pltpu.VMEM((LAG * SH, 2 * K), bf),
            pltpu.VMEM((NKB, 128), f4),
            pltpu.VMEM((LAG * SH, UR * WIN), f4),
            pltpu.VMEM((48, S2, 128), f4),
            pltpu.VMEM((8 * HR, 128), f4),
            pltpu.VMEM((8, HR, 128), bf),
            pltpu.VMEM((8, HR, 128), bf),
            pltpu.VMEM((48, 16, 128), bf),
            pltpu.VMEM((48, 16, 128), bf),
            pltpu.VMEM((16 * R, 128), f4),
            dma((NSEM,)), dma((NSEM,)), dma((4,)), dma((4,)), dma((2,)), dma((16,)), dma((16,)), dma((2,)),
        ],
        compiler_params=pltpu.CompilerParams(collective_id=0, has_side_effects=True,
                                             vmem_limit_bytes=60 * 1024 * 1024),
    )(gathered, shot_window, apertures.T, taper_index.T, taper_table)
    return jnp.transpose(out, (1, 0, 2))


def solution(mesh):
    in_specs = (P("shot", None, None), P("tm", "shot", None), P("shot", None), P("shot", None), P())
    out_specs = P("tm", "shot", None)
    return jax.shard_map(body, mesh=mesh, in_specs=in_specs, out_specs=out_specs, check_vma=False)
```

time: 212 us -> 58.8 us (0.28)
  waiting for transfers between devices: 141 us -> 0 us
  Pallas kernels: 0 us -> 56.4 us
  local copies, waits for them, and re-layouts: 28.8 us -> 1.77 us
  matrix products: 22.1 us -> 0 us
  between operations: 13.5 us -> 0.01 us
  other arithmetic: 3.39 us -> 0 us
    all_gather x1 -> x0, waiting for transfers between devices: 137 us -> none  [body(): lax.all_gather(receiver_data, 'shot', axis=1, tiled=True)]
    pallas_call x0 -> x1, Pallas kernels: none -> 56.4 us  [body(): pl.pallas_call(kernel, out_shape=jax.ShapeDtypeStruct((SH, TS, R), bf), i...]
    dot_general x1 -> x0, matrix products: 22.1 us -> none  [convolve_blocks(): jnp.einsum('sjck,bcnk->bjsn', banded, windows, preferred_element_type=jnp...]
    gather x1 -> x0, local copies, waits for them, and re-layouts: 18.9 us -> none  [toeplitz_operator(): spread = operator[:, clipped, :]]
    all_gather x1 -> x0, local copies, waits for them, and re-layouts: 6.35 us -> none  [body(): lax.all_gather(receiver_data, 'shot', axis=1, tiled=True)]
    ppermute x1 -> x0, waiting for transfers between devices: 3.5 us -> none  [from_behind(): lax.ppermute(value, axis, [(source, source + steps) for source in range(f...]
  transfers between devices with their start and end apart: 2 -> 0, of which waited for: 2 -> 0; matrix products, arithmetic and copies ran while one was open for 11% -> 0% of each run, Pallas kernels for 0% -> 0%
where the time goes in v1:
time: 58.8 us; the launch traced here: 58.2 us
  Pallas kernels  56.4 us (96%)
  local copies, waits for them, and re-layouts  1.77 us (3%)
    pallas_call x1, Pallas kernels, body(): pl.pallas_call(kernel, out_shape=jax.ShapeDtypeStruct((SH, TS, R), bf), i...  56.4 us
    unnamed x1, local copies, waits for them, and re-layouts  1.77 us

profile of v1, /device:TPU:1, one launch (start us, length us, event | category | flops | bytes accessed | tf_op | source)
XLA Modules:
  0.0 58.2 jit_solution(112441865118379279)
XLA Ops:
  0.0 56.4 %shard_map.55 = bf16[12,64,192]{2,1,0:T(8,128)(2,1)} custom-call(bf16[3,64,256]{2,1,0:T(8,128)(2,1)} %bitcast.5, bf16[12,32,256]{2,1,0:T(8,128)(2,1)} %shot_hbm.1, s32[4,12]{1,0:T(4,128)} %bitcast.6, s32[4,12]{1,0:T(4,128)} %bitcast.7, f32[16]{0:T(128)} %table_ref.1), custom_call_target="tpu_custom_call" | custom-call | tf_op jit(solution)/shard_map/pallas_call | solution.py:341
  56.4 1.8 %copy.7 = bf16[64,12,192]{2,0,1:T(8,128)(2,1)} copy(bf16[64,12,192]{2,0,1:T(8,128)(2,1)} %bitcast.4) | data formatting | bytes 589824

commit v2 on v1

--- a/solution.py
+++ b/solution.py
@@ -28,8 +28,8 @@
     return (((x * NH + h) * NY + y) * NC + c, t)
 
 
-def kernel(x_ref, shot_hbm, aper_ref, tidx_ref, table_ref, out_ref,
-           xg, rz, shot_ref, op_own, op_sib, op_f32, op_all, wt, prod, main, half_f32, halo_out, halo_in,
+def kernel(x_ref, shot_hbm, aper_hbm, tidx_hbm, table_hbm, out_ref,
+           xg, rz, aper_ref, tidx_ref, table_ref, shot_ref, op_own, op_sib, op_f32, op_all, wt, prod, main, half_f32, halo_out, halo_in,
            ex_out, ex_in, wide, send_sem, recv_sem, z_send, z_recv, op_sem, halo_sem, ex_sem, local_sem):
     shot_i = lax.axis_index("shot")
     t = lax.axis_index("tm")
@@ -55,19 +55,18 @@
     }
     partners = list(near.values()) + [up, down, sibling, after, before]
 
+    barrier = pltpu.get_barrier_semaphore()
+    for who in partners:
+        pl.semaphore_signal(barrier, inc=1, device_id=who, device_id_type=MESH)
     own_copy = pltpu.make_async_copy(x_ref, xg.at[0, x, pl.ds(ys[0], RC), pl.ds(HEAD, TS)], local_sem.at[0])
     own_copy.start()
     shot_copy = pltpu.make_async_copy(shot_hbm, shot_ref, local_sem.at[1])
     shot_copy.start()
-
-    for l in range(2):
-        xg[l, :, :, 0:HEAD, :] = jnp.zeros((NX, UR, HEAD, K), jnp.bfloat16)
-        xg[l, :, :, HEAD + TS:ROWS, :] = jnp.zeros((NX, UR, ROWS - HEAD - TS, K), jnp.bfloat16)
-    half_f32[...] = jnp.zeros_like(half_f32)
-
-    barrier = pltpu.get_barrier_semaphore()
-    for who in partners:
-        pl.semaphore_signal(barrier, inc=1, device_id=who, device_id_type=MESH)
+    small = [pltpu.make_async_copy(a, b, local_sem.at[2 + i])
+             for i, (a, b) in enumerate(((aper_hbm, aper_ref), (tidx_hbm, tidx_ref), (table_hbm, table_ref)))]
+    for copy in small:
+        copy.start()
+
     pl.semaphore_wait(barrier, len(partners))
 
     sends = []
@@ -151,15 +150,25 @@
                 recv(l, n, 2, off, HALF[n])
                 send(l, n, 2, off, piece[n], b, way)
 
+    def last(l, n, oa):
+        recv(l, n, oa, -2, PLUS[n])
+        recv(l, n, oa, 2, MINUS[n])
+
     def round4(l):
         for oa in (-1, 1, 2):
             for n in (0, 1):
-                recv(l, n, oa, -2, PLUS[n])
-                recv(l, n, oa, 2, MINUS[n])
+                last(l, n, oa)
 
     base(0, 0)
     base(0, 1)
 
+    for l in range(2):
+        xg[l, :, :, 0:HEAD, :] = jnp.zeros((NX, UR, HEAD, K), jnp.bfloat16)
+        xg[l, :, :, HEAD + TS:ROWS, :] = jnp.zeros((NX, UR, ROWS - HEAD - TS, K), jnp.bfloat16)
+    half_f32[...] = jnp.zeros_like(half_f32)
+
+    for copy in small:
+        copy.wait()
     wt[...] = jnp.zeros_like(wt)
     tidx = tidx_ref[...]
     aper = aper_ref[...]
@@ -300,14 +309,16 @@
     finish(2)
     round3(1)
     finish(3)
-    accept(0)
-    accept(1)
-    round4(1)
+    for g in range(4):
+        accept(g)
+    last(1, 1, 1)
     unit(5)
+    last(1, 1, -1)
     unit(6)
+    last(1, 1, 2)
+    for oa in (-1, 1, 2):
+        last(1, 0, oa)
     unit(7)
-    accept(2)
-    accept(3)
     for g in (4, 5, 6, 7):
         finish(g)
     for g in (4, 5, 6, 7):
@@ -341,11 +352,14 @@
     out = pl.pallas_call(
         kernel,
         out_shape=jax.ShapeDtypeStruct((SH, TS, R), bf),
-        in_specs=[pl.BlockSpec(memory_space=pl.ANY), pl.BlockSpec(memory_space=pl.ANY), vmem, vmem, pl.BlockSpec(memory_space=pltpu.SMEM)],
+        in_specs=[pl.BlockSpec(memory_space=pltpu.HBM)] * 5,
         out_specs=vmem,
         scratch_shapes=[
             pltpu.VMEM((2, NX, UR, ROWS, K), bf),
             pltpu.VMEM((2, RC, 32, K), bf),
+            pltpu.VMEM((4, SH), jnp.int32),
+            pltpu.VMEM((4, SH), jnp.int32),
+            pltpu.SMEM((16,), f4),
             pltpu.VMEM((SH, LAG, K), bf),
             pltpu.VMEM((SH, LAG, K), bf),
             pltpu.VMEM((SH, LAG, K), bf),
@@ -360,7 +374,7 @@
             pltpu.VMEM((48, 16, 128), bf),
             pltpu.VMEM((48, 16, 128), bf),
             pltpu.VMEM((16 * R, 128), f4),
-            dma((NSEM,)), dma((NSEM,)), dma((4,)), dma((4,)), dma((2,)), dma((16,)), dma((16,)), dma((2,)),
+            dma((NSEM,)), dma((NSEM,)), dma((4,)), dma((4,)), dma((2,)), dma((16,)), dma((16,)), dma((5,)),
         ],
         compiler_params=pltpu.CompilerParams(collective_id=0, has_side_effects=True,
                                              vmem_limit_bytes=60 * 1024 * 1024),

time: 58.8 us -> 56 us (0.952)
  Pallas kernels: 56.4 us -> 53.5 us
    pallas_call x1, Pallas kernels: 56.4 us -> 53.5 us  [body(): pl.pallas_call(kernel, out_shape=jax.ShapeDtypeStruct((SH, TS, R), bf), i...]
where the time goes in v2:
time: 56 us; the launch traced here: 55.2 us
  Pallas kernels  53.5 us (96%)
  local copies, waits for them, and re-layouts  1.77 us (3%)
    pallas_call x1, Pallas kernels, body(): pl.pallas_call(kernel, out_shape=jax.ShapeDtypeStruct((SH, TS, R), bf), i...  53.5 us
    unnamed x1, local copies, waits for them, and re-layouts  1.77 us

profile of v2, /device:TPU:1, one launch (start us, length us, event | category | flops | bytes accessed | tf_op | source)
XLA Modules:
  0.0 55.2 jit_solution(11647358168936508194)
XLA Ops:
  0.0 53.5 %shard_map.55 = bf16[12,64,192]{2,1,0:T(8,128)(2,1)} custom-call(bf16[3,64,256]{2,1,0:T(8,128)(2,1)} %bitcast.5, bf16[12,32,256]{2,1,0:T(8,128)(2,1)} %shot_hbm.1, s32[4,12]{1,0:T(4,128)} %bitcast.6, s32[4,12]{1,0:T(4,128)} %bitcast.7, f32[16]{0:T(128)} %table_hbm.1), custom_call_target="tpu_custom_call" | custom-call | tf_op jit(solution)/shard_map/pallas_call | solution.py:352
  53.5 1.8 %copy.7 = bf16[64,12,192]{2,0,1:T(8,128)(2,1)} copy(bf16[64,12,192]{2,0,1:T(8,128)(2,1)} %bitcast.4) | data formatting | bytes 589824

commit v3 on v2

--- a/solution.py
+++ b/solution.py
@@ -14,6 +14,7 @@
 UR = NY * RC
 NCH = 3
 R = 192
+STEP = 200
 HEAD, ROWS, WIN = 16, 112, 96
 ORDER = (0, 1, 3, 2)
 HR = 80
@@ -84,8 +85,9 @@
         sends.append(copy)
         return copy
 
-    z_first = [start(remote(x_ref.at[:, pl.ds(32 * d, 32)], rz.at[d], z_send.at[d], z_recv.at[d], who))
-               for d, who in ((0, up), (1, down))]
+    z_first = [[start(remote(x_ref.at[pl.ds(i, 1), pl.ds(32 * d, 32)], rz.at[d, pl.ds(i, 1)],
+                             z_send.at[2 * i + d], z_recv.at[2 * i + d], who))
+                for d, who in ((0, up), (1, down))] for i in range(RC)]
 
     def send(l, n, oa, ob, rows, axis, way):
         first = "y" if n == 0 else "x"
@@ -189,9 +191,12 @@
 
     round1(0)
     z_second = []
-    for d, who in ((0, up), (1, down)):
-        z_first[d].wait_recv()
-        z_second.append(start(remote(rz.at[d], slot(1, 0, 0, HALF[d]), z_send.at[2 + d], z_recv.at[2 + d], who)))
+    for i in range(RC):
+        for d, who in ((0, up), (1, down)):
+            z_first[i][d].wait_recv()
+            dst = xg.at[1, x, pl.ds(ys[0] + i, 1), pl.ds(HEAD + HALF[d][0], 32)]
+            k = 2 * (RC + i) + d
+            z_second.append(start(remote(rz.at[d, pl.ds(i, 1)], dst, z_send.at[k], z_recv.at[k], who)))
 
     def place(ref, s, row):
         v = ref[s].astype(jnp.float32)
@@ -248,8 +253,8 @@
             ry = 4 * j + ((0, 1), (3, 2))[q][k]
             row = rows_of[g % 4] + 24 * ((h + g // 4) % 2) + core * 3 + (ry // 3) * 6 + ry % 3
             mask = (lane8 < 64) if k == 0 else (lane8 >= 64)
-            wide[pl.ds(base_s * R + row, 8, stride=R), :] = jnp.where(mask, second8, 0.0)
-            wide[pl.ds(row, 8, stride=R), :] = jnp.where(mask, first8, 0.0)
+            wide[pl.ds(base_s * STEP + row, 8, stride=STEP), :] = jnp.where(mask, second8, 0.0)
+            wide[pl.ds(row, 8, stride=STEP), :] = jnp.where(mask, first8, 0.0)
 
     def exchange_copy(g):
         rows = pl.ds(g * 2 * NCH, 2 * NCH)
@@ -295,7 +300,8 @@
     unit(0)
     round3(0)
     for n in (0, 1):
-        z_second[n].wait_recv()
+        for i in range(RC):
+            z_second[2 * i + n].wait_recv()
         base(1, n)
     round4(0)
     unit(1)
@@ -315,20 +321,23 @@
     unit(5)
     last(1, 1, -1)
     unit(6)
+    finish(4)
     last(1, 1, 2)
     for oa in (-1, 1, 2):
         last(1, 0, oa)
     unit(7)
-    for g in (4, 5, 6, 7):
+    for g in (5, 6):
         finish(g)
-    for g in (4, 5, 6, 7):
+    accept(4)
+    finish(7)
+    for g in (5, 6, 7):
         accept(g)
 
     both = lax.broadcasted_iota(jnp.int32, (TS, 128), 1) % TS == lax.broadcasted_iota(jnp.int32, (TS, 128), 0)
     both = jnp.where(both, 1.0, 0.0).astype(jnp.bfloat16)
 
     def turn(s, carry):
-        block = wide[pl.ds(pl.multiple_of(s * R, 8), R), :].astype(jnp.bfloat16)
+        block = wide[pl.ds(pl.multiple_of(s * STEP, 8), R), :].astype(jnp.bfloat16)
         out_ref[s] = lax.dot_general(both, block, (((1,), (1,)), ((), ())),
                                      preferred_element_type=jnp.float32).astype(jnp.bfloat16)
         return carry
@@ -373,8 +382,8 @@
             pltpu.VMEM((8, HR, 128), bf),
             pltpu.VMEM((48, 16, 128), bf),
             pltpu.VMEM((48, 16, 128), bf),
-            pltpu.VMEM((16 * R, 128), f4),
-            dma((NSEM,)), dma((NSEM,)), dma((4,)), dma((4,)), dma((2,)), dma((16,)), dma((16,)), dma((5,)),
+            pltpu.VMEM((16 * STEP, 128), f4),
+            dma((NSEM,)), dma((NSEM,)), dma((4 * RC,)), dma((4 * RC,)), dma((2,)), dma((16,)), dma((16,)), dma((5,)),
         ],
         compiler_params=pltpu.CompilerParams(collective_id=0, has_side_effects=True,
                                              vmem_limit_bytes=60 * 1024 * 1024),

time: 56 us -> 56 us (level)
  no operation moved by 1% of the time
where the time goes in v3:
time: 56 us; the launch traced here: 55.2 us
  Pallas kernels  53.4 us (95%)
  local copies, waits for them, and re-layouts  1.77 us (3%)
    pallas_call x1, Pallas kernels, body(): pl.pallas_call(kernel, out_shape=jax.ShapeDtypeStruct((SH, TS, R), bf), i...  53.4 us
    unnamed x1, local copies, waits for them, and re-layouts  1.77 us

profile of v3, /device:TPU:1, one launch (start us, length us, event | category | flops | bytes accessed | tf_op | source)
XLA Modules:
  0.0 55.2 jit_solution(531416679953774358)
XLA Ops:
  0.0 53.4 %shard_map.55 = bf16[12,64,192]{2,1,0:T(8,128)(2,1)} custom-call(bf16[3,64,256]{2,1,0:T(8,128)(2,1)} %bitcast.5, bf16[12,32,256]{2,1,0:T(8,128)(2,1)} %shot_hbm.1, s32[4,12]{1,0:T(4,128)} %bitcast.6, s32[4,12]{1,0:T(4,128)} %bitcast.7, f32[16]{0:T(128)} %table_hbm.1), custom_call_target="tpu_custom_call" | custom-call | tf_op jit(solution)/shard_map/pallas_call | solution.py:361
  53.4 1.8 %copy.7 = bf16[64,12,192]{2,0,1:T(8,128)(2,1)} copy(bf16[64,12,192]{2,0,1:T(8,128)(2,1)} %bitcast.4) | data formatting | bytes 589824

commit v4 on v3

--- a/solution.py
+++ b/solution.py
@@ -31,7 +31,7 @@
 
 def kernel(x_ref, shot_hbm, aper_hbm, tidx_hbm, table_hbm, out_ref,
            xg, rz, aper_ref, tidx_ref, table_ref, shot_ref, op_own, op_sib, op_f32, op_all, wt, prod, main, half_f32, halo_out, halo_in,
-           ex_out, ex_in, wide, send_sem, recv_sem, z_send, z_recv, op_sem, halo_sem, ex_sem, local_sem):
+           ex_out, ex_in, wide, result, send_sem, recv_sem, z_send, z_recv, op_sem, halo_sem, ex_sem, out_sem, local_sem):
     shot_i = lax.axis_index("shot")
     t = lax.axis_index("tm")
     c = shot_i % 2
@@ -85,6 +85,10 @@
         sends.append(copy)
         return copy
 
+    def flush(keep):
+        while len(sends) > keep:
+            sends.pop(0).wait_send()
+
     z_first = [[start(remote(x_ref.at[pl.ds(i, 1), pl.ds(32 * d, 32)], rz.at[d, pl.ds(i, 1)],
                              z_send.at[2 * i + d], z_recv.at[2 * i + d], who))
                 for d, who in ((0, up), (1, down))] for i in range(RC)]
@@ -313,10 +317,12 @@
     round2(1)
     unit(4)
     finish(2)
+    flush(20)
     round3(1)
     finish(3)
     for g in range(4):
         accept(g)
+    flush(8)
     last(1, 1, 1)
     unit(5)
     last(1, 1, -1)
@@ -336,16 +342,18 @@
     both = lax.broadcasted_iota(jnp.int32, (TS, 128), 1) % TS == lax.broadcasted_iota(jnp.int32, (TS, 128), 0)
     both = jnp.where(both, 1.0, 0.0).astype(jnp.bfloat16)
 
-    def turn(s, carry):
-        block = wide[pl.ds(pl.multiple_of(s * STEP, 8), R), :].astype(jnp.bfloat16)
-        out_ref[s] = lax.dot_general(both, block, (((1,), (1,)), ((), ())),
-                                     preferred_element_type=jnp.float32).astype(jnp.bfloat16)
-        return carry
-
-    lax.fori_loop(0, SH, turn, 0)
-
-    for copy in sends:
-        copy.wait_send()
+    leaving = []
+    for s in range(SH):
+        block = wide[s * STEP:s * STEP + R, :].astype(jnp.bfloat16)
+        result[s] = lax.dot_general(both, block, (((1,), (1,)), ((), ())),
+                                    preferred_element_type=jnp.float32).astype(jnp.bfloat16)
+        copy = pltpu.make_async_copy(result.at[s], out_ref.at[s], out_sem.at[s])
+        copy.start()
+        leaving.append(copy)
+
+    flush(0)
+    for copy in leaving:
+        copy.wait()
 
     @pl.when(t < NTM - 1)
     def _():
@@ -355,14 +363,13 @@
 
 def body(shot_window, receiver_data, apertures, taper_index, taper_table):
     gathered = jnp.transpose(receiver_data, (1, 0, 2))
-    vmem = pl.BlockSpec(memory_space=pltpu.VMEM)
     bf, f4 = jnp.bfloat16, jnp.float32
     dma = pltpu.SemaphoreType.DMA
     out = pl.pallas_call(
         kernel,
         out_shape=jax.ShapeDtypeStruct((SH, TS, R), bf),
         in_specs=[pl.BlockSpec(memory_space=pltpu.HBM)] * 5,
-        out_specs=vmem,
+        out_specs=pl.BlockSpec(memory_space=pl.ANY),
         scratch_shapes=[
             pltpu.VMEM((2, NX, UR, ROWS, K), bf),
             pltpu.VMEM((2, RC, 32, K), bf),
@@ -383,7 +390,8 @@
             pltpu.VMEM((48, 16, 128), bf),
             pltpu.VMEM((48, 16, 128), bf),
             pltpu.VMEM((16 * STEP, 128), f4),
-            dma((NSEM,)), dma((NSEM,)), dma((4 * RC,)), dma((4 * RC,)), dma((2,)), dma((16,)), dma((16,)), dma((5,)),
+            pltpu.VMEM((SH, TS, R), bf),
+            dma((NSEM,)), dma((NSEM,)), dma((4 * RC,)), dma((4 * RC,)), dma((2,)), dma((16,)), dma((16,)), dma((SH,)), dma((5,)),
         ],
         compiler_params=pltpu.CompilerParams(collective_id=0, has_side_effects=True,
                                              vmem_limit_bytes=60 * 1024 * 1024),

time: 56 us -> 54.1 us (0.966)
  Pallas kernels: 53.4 us -> 51.6 us
    pallas_call x1, Pallas kernels: 53.4 us -> 51.6 us  [body(): pl.pallas_call(kernel, out_shape=jax.ShapeDtypeStruct((SH, TS, R), bf), i...]
where the time goes in v4:
time: 54.1 us; the launch traced here: 53.3 us
  Pallas kernels  51.6 us (95%)
  local copies, waits for them, and re-layouts  1.77 us (3%)
    pallas_call x1, Pallas kernels, body(): pl.pallas_call(kernel, out_shape=jax.ShapeDtypeStruct((SH, TS, R), bf), i...  51.6 us
    unnamed x1, local copies, waits for them, and re-layouts  1.77 us

profile of v4, /device:TPU:1, one launch (start us, length us, event | category | flops | bytes accessed | tf_op | source)
XLA Modules:
  0.0 53.3 jit_solution(3724121032325732398)
XLA Ops:
  0.0 51.6 %shard_map.55 = bf16[12,64,192]{2,1,0:T(8,128)(2,1)} custom-call(bf16[3,64,256]{2,1,0:T(8,128)(2,1)} %bitcast.5, bf16[12,32,256]{2,1,0:T(8,128)(2,1)} %shot_hbm.1, s32[4,12]{1,0:T(4,128)} %bitcast.6, s32[4,12]{1,0:T(4,128)} %bitcast.7, f32[16]{0:T(128)} %table_hbm.1), custom_call_target="tpu_custom_call" | custom-call | tf_op jit(solution)/shard_map/pallas_call | solution.py:368
  51.6 1.8 %copy.7 = bf16[64,12,192]{2,0,1:T(8,128)(2,1)} copy(bf16[64,12,192]{2,0,1:T(8,128)(2,1)} %bitcast.4) | data formatting | bytes 589824

commit v5 on v4

--- a/solution.py
+++ b/solution.py
@@ -40,7 +40,7 @@
     x = shot_i // 16
     z = h * NTM + t
     xs = [(x + d) % NX for d in range(NX)]
-    ys = [RC * ((y + d) % NY) for d in range(NY)]
+    ys = [(y + d) % NY for d in range(NY)]
     zp = (z + 4) % NZ
     zm = (z + NZ - 4) % NZ
     up = device(x, y, zp // NTM, c, zp % NTM)
@@ -54,12 +54,14 @@
         ("y", 1): device(x, (y + 1) % NY, h, c, t),
         ("y", -1): device(x, (y + NY - 1) % NY, h, c, t),
     }
-    partners = list(near.values()) + [up, down, sibling, after, before]
+    cross_after = device(x, y, h, 1 - c, (t + 1) % NTM)
+    cross_before = device(x, y, h, 1 - c, (t + NTM - 1) % NTM)
+    partners = list(near.values()) + [up, down, sibling, after, before, cross_after, cross_before]
 
     barrier = pltpu.get_barrier_semaphore()
     for who in partners:
         pl.semaphore_signal(barrier, inc=1, device_id=who, device_id_type=MESH)
-    own_copy = pltpu.make_async_copy(x_ref, xg.at[0, x, pl.ds(ys[0], RC), pl.ds(HEAD, TS)], local_sem.at[0])
+    own_copy = pltpu.make_async_copy(x_ref, xg.at[0, 0, pl.ds(0, RC), pl.ds(HEAD, TS)], local_sem.at[0])
     own_copy.start()
     shot_copy = pltpu.make_async_copy(shot_hbm, shot_ref, local_sem.at[1])
     shot_copy.start()
@@ -74,7 +76,7 @@
     kinds = {}
 
     def slot(l, dx, dy, rows):
-        return xg.at[l, xs[dx % NX], pl.ds(ys[dy % NY], RC), pl.ds(HEAD + rows[0], rows[1])]
+        return xg.at[l, dx % NX, pl.ds(RC * (dy % NY), RC), pl.ds(HEAD + rows[0], rows[1])]
 
     def remote(src, dst, ssem, rsem, who):
         return pltpu.make_async_remote_copy(src_ref=src, dst_ref=dst, send_sem=ssem, recv_sem=rsem,
@@ -100,11 +102,12 @@
         other = way if axis != first else 0
         key = (l, n, oa - step, ob - other, rows)
         k = kinds.setdefault(("sem",) + key + (axis, way), len([q for q in kinds if q[0] == "sem"]))
-        ref = slot(l, dx, dy, rows)
-        src = ref
+        src = slot(l, dx, dy, rows)
         if l == 0 and oa == 0 and ob == 0:
             src = x_ref.at[:, pl.ds(rows[0], rows[1])]
-        kinds[key] = start(remote(src, ref, send_sem.at[k], recv_sem.at[k], near[(axis, way)]))
+        back = (-way, 0) if axis == "x" else (0, -way)
+        dst = slot(l, dx + back[0], dy + back[1], rows)
+        kinds[key] = start(remote(src, dst, send_sem.at[k], recv_sem.at[k], near[(axis, way)]))
 
     def recv(l, n, oa, ob, rows):
         kinds[(l, n, oa, ob, rows)].wait_recv()
@@ -172,6 +175,10 @@
         xg[l, :, :, 0:HEAD, :] = jnp.zeros((NX, UR, HEAD, K), jnp.bfloat16)
         xg[l, :, :, HEAD + TS:ROWS, :] = jnp.zeros((NX, UR, ROWS - HEAD - TS, K), jnp.bfloat16)
     half_f32[...] = jnp.zeros_like(half_f32)
+
+    @pl.when(t == 0)
+    def _():
+        halo_in[...] = jnp.zeros_like(halo_in)
 
     for copy in small:
         copy.wait()
@@ -198,7 +205,7 @@
     for i in range(RC):
         for d, who in ((0, up), (1, down)):
             z_first[i][d].wait_recv()
-            dst = xg.at[1, x, pl.ds(ys[0] + i, 1), pl.ds(HEAD + HALF[d][0], 32)]
+            dst = xg.at[1, 0, pl.ds(i, 1), pl.ds(HEAD + HALF[d][0], 32)]
             k = 2 * (RC + i) + d
             z_second.append(start(remote(rz.at[d, pl.ds(i, 1)], dst, z_send.at[k], z_recv.at[k], who)))
 
@@ -220,7 +227,7 @@
     lane = lax.broadcasted_iota(jnp.int32, (S2, 128), 1)
 
     def compute(g):
-        l, ux = g // 4, xs[ORDER[g % 4]]
+        l, ux = g // 4, ORDER[g % 4]
         for r0, nr in ((0, 8), (8, 4)):
             late = xg[l, ux, r0:r0 + nr, HEAD:HEAD + WIN, :].reshape(nr * WIN, K)
             early = xg[l, ux, r0:r0 + nr, 0:WIN, :].reshape(nr * WIN, K)
@@ -233,20 +240,25 @@
                 acc = acc + pltpu.roll(prod[b * S2:(b + 1) * S2, j * 4 * WIN:(j + 1) * 4 * WIN], b, 1)
             v0, v1, v2 = acc[:, 0:128], acc[:, 128:256], acc[:, 256:384]
             index = g * NCH + j
-            main[2 * index] = jnp.where(lane < 64, v0, pltpu.roll(jnp.where(lane >= 96, v0, v1), 96, 1))
-            main[2 * index + 1] = jnp.where(lane < 64, pltpu.roll(v2, 96, 1), v1)
+            pairs = (jnp.where(lane < 64, v0, pltpu.roll(jnp.where(lane >= 96, v0, v1), 96, 1)),
+                     jnp.where(lane < 64, pltpu.roll(v2, 96, 1), v1))
+            for q in range(2):
+                main[2 * index + q] = pairs[q]
+                ex_out[2 * index + q] = pairs[q][8:24]
             halo = jnp.where(lane < 32, v2, jnp.where(lane < 64, v1, jnp.where(lane < 96, v0, v2)))
             half_f32[g * HR + j * S2:g * HR + (j + 1) * S2, :] = halo
 
-    def halo_copy(g):
-        return remote(halo_out.at[g], halo_in.at[g], halo_sem.at[g], halo_sem.at[8 + g], after)
+    def halo_copy(g, k):
+        return remote(halo_out.at[g], halo_in.at[k, g], halo_sem.at[16 * k + g], halo_sem.at[16 * k + 8 + g],
+                      (after, cross_after)[k])
 
     def send_halo(g):
         halo_out[g] = half_f32[g * HR:(g + 1) * HR, :].astype(jnp.bfloat16)
 
         @pl.when(t < NTM - 1)
         def _():
-            halo_copy(g).start()
+            for k in range(2):
+                halo_copy(g, k).start()
 
     lane8 = lax.broadcasted_iota(jnp.int32, (8, 128), 1)
 
@@ -255,7 +267,7 @@
     def widen(g, j, q, first8, second8, base_s, core):
         for k in range(2):
             ry = 4 * j + ((0, 1), (3, 2))[q][k]
-            row = rows_of[g % 4] + 24 * ((h + g // 4) % 2) + core * 3 + (ry // 3) * 6 + ry % 3
+            row = rows_of[g % 4] + 24 * ((h + g // 4) % 2) + core * 3 + 6 * ys[ry // 3] + ry % 3
             mask = (lane8 < 64) if k == 0 else (lane8 >= 64)
             wide[pl.ds(base_s * STEP + row, 8, stride=STEP), :] = jnp.where(mask, second8, 0.0)
             wide[pl.ds(row, 8, stride=STEP), :] = jnp.where(mask, first8, 0.0)
@@ -266,38 +278,32 @@
 
     copies = {}
 
-    def finish(g):
+    def close(g):
         @pl.when(t > 0)
         def _():
-            halo_copy(g).wait_recv()
-            half_f32[g * HR:(g + 1) * HR, :] = halo_in[g].astype(jnp.float32)
-
-        @pl.when(t == 0)
-        def _():
-            half_f32[g * HR:(g + 1) * HR, :] = jnp.zeros((HR, 128), jnp.float32)
-
-        for j in range(NCH):
-            packed = half_f32[g * HR + j * S2:g * HR + (j + 1) * S2, :]
-            by32, by64 = pltpu.roll(packed, 32, 1), pltpu.roll(packed, 64, 1)
-            for q in range(2):
-                index = 2 * (g * NCH + j) + q
-                part = jnp.where(lane < 64, by64, by32) if q == 0 else jnp.where(lane < 64, by32, by64)
-                v = main[index] + jnp.where(lane % 64 < 32, part, 0.0)
-                v = v.astype(jnp.bfloat16).astype(jnp.float32)
-                ex_out[index] = v[8:24].astype(jnp.bfloat16)
-                widen(g, j, q, v[0:8], v[16:24], 8, c)
-        copies[g] = start(exchange_copy(g))
-
-    def accept(g):
+            for k in range(2):
+                halo_copy(g, k).wait_recv()
+
         copies[g].wait_recv()
-        for j in range(NCH):
-            for q in range(2):
-                v = ex_in[2 * (g * NCH + j) + q].astype(jnp.float32)
-                widen(g, j, q, v[0:8], v[8:16], 4, 1 - c)
+        for k in range(2):
+            halo = halo_in[k, g].astype(jnp.float32)
+            for j in range(NCH):
+                packed = halo[j * S2 + 8 * k:(j + 1) * S2]
+                place = lane[8 * k:]
+                by32, by64 = pltpu.roll(packed, 32, 1), pltpu.roll(packed, 64, 1)
+                for q in range(2):
+                    index = 2 * (g * NCH + j) + q
+                    part = jnp.where(place < 64, by64, by32) if q == 0 else jnp.where(place < 64, by32, by64)
+                    v = (main, ex_in)[k][index] + jnp.where(place % 64 < 32, part, 0.0)
+                    if k == 0:
+                        widen(g, j, q, v[0:8], v[16:24], 8, c)
+                    else:
+                        widen(g, j, q, v[0:8], v[8:16], 4, 1 - c)
 
     def unit(g):
         compute(g)
         send_halo(g)
+        copies[g] = start(exchange_copy(g))
 
     round2(0)
     own_copy.wait()
@@ -312,32 +318,26 @@
     unit(2)
     round1(1)
     unit(3)
-    finish(0)
-    finish(1)
+    close(0)
+    close(1)
     round2(1)
     unit(4)
-    finish(2)
+    close(2)
     flush(20)
     round3(1)
-    finish(3)
-    for g in range(4):
-        accept(g)
+    close(3)
     flush(8)
     last(1, 1, 1)
     unit(5)
     last(1, 1, -1)
     unit(6)
-    finish(4)
+    close(4)
     last(1, 1, 2)
     for oa in (-1, 1, 2):
         last(1, 0, oa)
     unit(7)
-    for g in (5, 6):
-        finish(g)
-    accept(4)
-    finish(7)
     for g in (5, 6, 7):
-        accept(g)
+        close(g)
 
     both = lax.broadcasted_iota(jnp.int32, (TS, 128), 1) % TS == lax.broadcasted_iota(jnp.int32, (TS, 128), 0)
     both = jnp.where(both, 1.0, 0.0).astype(jnp.bfloat16)
@@ -358,7 +358,8 @@
     @pl.when(t < NTM - 1)
     def _():
         for g in range(8):
-            halo_copy(g).wait_send()
+            for k in range(2):
+                halo_copy(g, k).wait_send()
 
 
 def body(shot_window, receiver_data, apertures, taper_index, taper_table):
@@ -386,12 +387,12 @@
             pltpu.VMEM((48, S2, 128), f4),
             pltpu.VMEM((8 * HR, 128), f4),
             pltpu.VMEM((8, HR, 128), bf),
-            pltpu.VMEM((8, HR, 128), bf),
-            pltpu.VMEM((48, 16, 128), bf),
-            pltpu.VMEM((48, 16, 128), bf),
+            pltpu.VMEM((2, 8, HR, 128), bf),
+            pltpu.VMEM((48, 16, 128), f4),
+            pltpu.VMEM((48, 16, 128), f4),
             pltpu.VMEM((16 * STEP, 128), f4),
             pltpu.VMEM((SH, TS, R), bf),
-            dma((NSEM,)), dma((NSEM,)), dma((4 * RC,)), dma((4 * RC,)), dma((2,)), dma((16,)), dma((16,)), dma((SH,)), dma((5,)),
+            dma((NSEM,)), dma((NSEM,)), dma((4 * RC,)), dma((4 * RC,)), dma((2,)), dma((32,)), dma((16,)), dma((SH,)), dma((5,)),
         ],
         compiler_params=pltpu.CompilerParams(collective_id=0, has_side_effects=True,
                                              vmem_limit_bytes=60 * 1024 * 1024),

time: 54.1 us -> 53.3 us (0.985); the launches traced: 53.3 us -> 53.2 us
  no operation moved by 1% of the time
where the time goes in v5:
time: 53.3 us; the launch traced here: 53.2 us
  Pallas kernels  51.4 us (96%)
  local copies, waits for them, and re-layouts  1.77 us (3%)
    pallas_call x1, Pallas kernels, body(): pl.pallas_call(kernel, out_shape=jax.ShapeDtypeStruct((SH, TS, R), bf), i...  51.4 us
    unnamed x1, local copies, waits for them, and re-layouts  1.77 us

profile of v5, /device:TPU:1, one launch (start us, length us, event | category | flops | bytes accessed | tf_op | source)
XLA Modules:
  0.0 53.2 jit_solution(8968713227646085240)
XLA Ops:
  0.0 51.4 %shard_map.55 = bf16[12,64,192]{2,1,0:T(8,128)(2,1)} custom-call(bf16[3,64,256]{2,1,0:T(8,128)(2,1)} %bitcast.5, bf16[12,32,256]{2,1,0:T(8,128)(2,1)} %shot_hbm.1, s32[4,12]{1,0:T(4,128)} %bitcast.6, s32[4,12]{1,0:T(4,128)} %bitcast.7, f32[16]{0:T(128)} %table_hbm.1), custom_call_target="tpu_custom_call" | custom-call | tf_op jit(solution)/shard_map/pallas_call | solution.py:369
  51.4 1.8 %copy.7 = bf16[64,12,192]{2,0,1:T(8,128)(2,1)} copy(bf16[64,12,192]{2,0,1:T(8,128)(2,1)} %bitcast.4) | data formatting | bytes 589824

commit v6 on v5

--- a/solution.py
+++ b/solution.py
@@ -200,14 +200,19 @@
         op_own[s] = (shot_ref[s].astype(jnp.float32) * spread[s:s + 1, :]).astype(jnp.bfloat16)
     op_copy = start(remote(op_own, op_sib, op_sem.at[0], op_sem.at[1], sibling))
 
-    round1(0)
     z_second = []
-    for i in range(RC):
+
+    def relay(i):
         for d, who in ((0, up), (1, down)):
             z_first[i][d].wait_recv()
             dst = xg.at[1, 0, pl.ds(i, 1), pl.ds(HEAD + HALF[d][0], 32)]
             k = 2 * (RC + i) + d
             z_second.append(start(remote(rz.at[d, pl.ds(i, 1)], dst, z_send.at[k], z_recv.at[k], who)))
+
+    relay(0)
+    round1(0)
+    relay(1)
+    relay(2)
 
     def place(ref, s, row):
         v = ref[s].astype(jnp.float32)
@@ -308,11 +313,11 @@
     round2(0)
     own_copy.wait()
     unit(0)
-    round3(0)
     for n in (0, 1):
         for i in range(RC):
             z_second[2 * i + n].wait_recv()
         base(1, n)
+    round3(0)
     round4(0)
     unit(1)
     unit(2)
@@ -345,8 +350,7 @@
     leaving = []
     for s in range(SH):
         block = wide[s * STEP:s * STEP + R, :].astype(jnp.bfloat16)
-        result[s] = lax.dot_general(both, block, (((1,), (1,)), ((), ())),
-                                    preferred_element_type=jnp.float32).astype(jnp.bfloat16)
+        result[s] = lax.dot_general(both, block, (((1,), (1,)), ((), ())), preferred_element_type=jnp.float32)
         copy = pltpu.make_async_copy(result.at[s], out_ref.at[s], out_sem.at[s])
         copy.start()
         leaving.append(copy)
@@ -368,7 +372,7 @@
     dma = pltpu.SemaphoreType.DMA
     out = pl.pallas_call(
         kernel,
-        out_shape=jax.ShapeDtypeStruct((SH, TS, R), bf),
+        out_shape=jax.ShapeDtypeStruct((SH, TS, R), f4),
         in_specs=[pl.BlockSpec(memory_space=pltpu.HBM)] * 5,
         out_specs=pl.BlockSpec(memory_space=pl.ANY),
         scratch_shapes=[
@@ -391,13 +395,13 @@
             pltpu.VMEM((48, 16, 128), f4),
             pltpu.VMEM((48, 16, 128), f4),
             pltpu.VMEM((16 * STEP, 128), f4),
-            pltpu.VMEM((SH, TS, R), bf),
+            pltpu.VMEM((SH, TS, R), f4),
             dma((NSEM,)), dma((NSEM,)), dma((4 * RC,)), dma((4 * RC,)), dma((2,)), dma((32,)), dma((16,)), dma((SH,)), dma((5,)),
         ],
         compiler_params=pltpu.CompilerParams(collective_id=0, has_side_effects=True,
                                              vmem_limit_bytes=60 * 1024 * 1024),
     )(gathered, shot_window, apertures.T, taper_index.T, taper_table)
-    return jnp.transpose(out, (1, 0, 2))
+    return jnp.transpose(out, (1, 0, 2)).astype(bf)
 
 
 def solution(mesh):

time: 53.3 us -> 56.5 us (1.060)
  Pallas kernels: 51.4 us -> 54.5 us
  other arithmetic: 0 us -> 1.93 us
  local copies, waits for them, and re-layouts: 1.77 us -> 0 us
    pallas_call x1, Pallas kernels: 51.4 us -> 54.5 us  [body(): pl.pallas_call(kernel, out_shape=jax.ShapeDtypeStruct((SH, TS, R), f4), i...]
    convert_element_type x0 -> x1, other arithmetic: none -> 1.93 us  [body(): return jnp.transpose(out, (1, 0, 2)).astype(bf)]
    unnamed x1 -> x0, local copies, waits for them, and re-layouts: 1.77 us -> none
where the time goes in v6:
time: 56.5 us; the launch traced here: 56.4 us
  Pallas kernels  54.5 us (96%)
  other arithmetic  1.93 us (3%)
    pallas_call x1, Pallas kernels, body(): pl.pallas_call(kernel, out_shape=jax.ShapeDtypeStruct((SH, TS, R), f4), i...  54.5 us
    convert_element_type x1, other arithmetic, body(): return jnp.transpose(out, (1, 0, 2)).astype(bf)  1.93 us

profile of v6, /device:TPU:1, one launch (start us, length us, event | category | flops | bytes accessed | tf_op | source)
XLA Modules:
  0.0 56.4 jit_solution(12055383651461802127)
XLA Ops:
  0.0 54.5 %shard_map.55 = f32[12,64,192]{2,1,0:T(8,128)} custom-call(bf16[3,64,256]{2,1,0:T(8,128)(2,1)} %bitcast.5, bf16[12,32,256]{2,1,0:T(8,128)(2,1)} %shot_hbm.1, s32[4,12]{1,0:T(4,128)} %bitcast.6, s32[4,12]{1,0:T(4,128)} %bitcast.7, f32[16]{0:T(128)} %table_hbm.1), custom_call_target="tpu_custom_call" | custom-call | tf_op jit(solution)/shard_map/pallas_call | solution.py:373
  54.5 1.9 %convert_bitcast_fusion = bf16[64,12,192]{2,0,1:T(8,128)(2,1)} fusion(f32[12,64,192]{2,1,0:T(8,128)} %shard_map.55), kind=kLoop, calls=%fused_computation | loop fusion | flops 147456 | bytes 884736 | tf_op jit(solution)/shard_map/convert_element_type | solution.py:404

commit v7 on v5

--- a/solution.py
+++ b/solution.py
@@ -7,7 +7,6 @@
 
 MESH = pl.DeviceIdType.MESH
 NX, NY, NH, NC, NTM = 4, 4, 2, 2, 8
-NZ = NH * NTM
 NKB, LAG, K = 8, 32, 256
 SH, RC, TS = 12, 3, 64
 S2 = 2 * SH
@@ -30,7 +29,7 @@
 
 
 def kernel(x_ref, shot_hbm, aper_hbm, tidx_hbm, table_hbm, out_ref,
-           xg, rz, aper_ref, tidx_ref, table_ref, shot_ref, op_own, op_sib, op_f32, op_all, wt, prod, main, half_f32, halo_out, halo_in,
+           xg, aper_ref, tidx_ref, table_ref, shot_ref, op_own, op_sib, op_f32, op_all, wt, prod, main, half_f32, halo_out, halo_in,
            ex_out, ex_in, wide, result, send_sem, recv_sem, z_send, z_recv, op_sem, halo_sem, ex_sem, out_sem, local_sem):
     shot_i = lax.axis_index("shot")
     t = lax.axis_index("tm")
@@ -38,13 +37,9 @@
     y = (shot_i // 2) % 4
     h = (shot_i // 8) % 2
     x = shot_i // 16
-    z = h * NTM + t
     xs = [(x + d) % NX for d in range(NX)]
     ys = [(y + d) % NY for d in range(NY)]
-    zp = (z + 4) % NZ
-    zm = (z + NZ - 4) % NZ
-    up = device(x, y, zp // NTM, c, zp % NTM)
-    down = device(x, y, zm // NTM, c, zm % NTM)
+    across = device(x, y, 1 - h, c, t)
     sibling = device(x, y, h, 1 - c, t)
     after = device(x, y, h, c, (t + 1) % NTM)
     before = device(x, y, h, c, (t + NTM - 1) % NTM)
@@ -56,7 +51,7 @@
     }
     cross_after = device(x, y, h, 1 - c, (t + 1) % NTM)
     cross_before = device(x, y, h, 1 - c, (t + NTM - 1) % NTM)
-    partners = list(near.values()) + [up, down, sibling, after, before, cross_after, cross_before]
+    partners = list(near.values()) + [across, sibling, after, before, cross_after, cross_before]
 
     barrier = pltpu.get_barrier_semaphore()
     for who in partners:
@@ -91,9 +86,9 @@
         while len(sends) > keep:
             sends.pop(0).wait_send()
 
-    z_first = [[start(remote(x_ref.at[pl.ds(i, 1), pl.ds(32 * d, 32)], rz.at[d, pl.ds(i, 1)],
-                             z_send.at[2 * i + d], z_recv.at[2 * i + d], who))
-                for d, who in ((0, up), (1, down))] for i in range(RC)]
+    z_copies = [start(remote(x_ref.at[pl.ds(i, 1), pl.ds(32 * n, 32)], xg.at[1, 0, pl.ds(i, 1), pl.ds(HEAD + 32 * n, 32)],
+                             z_send.at[n * RC + i], z_recv.at[n * RC + i], across))
+                for n in range(2) for i in range(RC)]
 
     def send(l, n, oa, ob, rows, axis, way):
         first = "y" if n == 0 else "x"
@@ -170,15 +165,6 @@
 
     base(0, 0)
     base(0, 1)
-
-    for l in range(2):
-        xg[l, :, :, 0:HEAD, :] = jnp.zeros((NX, UR, HEAD, K), jnp.bfloat16)
-        xg[l, :, :, HEAD + TS:ROWS, :] = jnp.zeros((NX, UR, ROWS - HEAD - TS, K), jnp.bfloat16)
-    half_f32[...] = jnp.zeros_like(half_f32)
-
-    @pl.when(t == 0)
-    def _():
-        halo_in[...] = jnp.zeros_like(halo_in)
 
     for copy in small:
         copy.wait()
@@ -201,13 +187,14 @@
     op_copy = start(remote(op_own, op_sib, op_sem.at[0], op_sem.at[1], sibling))
 
     round1(0)
-    z_second = []
-    for i in range(RC):
-        for d, who in ((0, up), (1, down)):
-            z_first[i][d].wait_recv()
-            dst = xg.at[1, 0, pl.ds(i, 1), pl.ds(HEAD + HALF[d][0], 32)]
-            k = 2 * (RC + i) + d
-            z_second.append(start(remote(rz.at[d, pl.ds(i, 1)], dst, z_send.at[k], z_recv.at[k], who)))
+    for l in range(2):
+        xg[l, :, :, 0:HEAD, :] = jnp.zeros((NX, UR, HEAD, K), jnp.bfloat16)
+        xg[l, :, :, HEAD + TS:ROWS, :] = jnp.zeros((NX, UR, ROWS - HEAD - TS, K), jnp.bfloat16)
+    half_f32[...] = jnp.zeros_like(half_f32)
+
+    @pl.when(t == 0)
+    def _():
+        halo_in[...] = jnp.zeros_like(halo_in)
 
     def place(ref, s, row):
         v = ref[s].astype(jnp.float32)
@@ -311,7 +298,7 @@
     round3(0)
     for n in (0, 1):
         for i in range(RC):
-            z_second[2 * i + n].wait_recv()
+            z_copies[n * RC + i].wait_recv()
         base(1, n)
     round4(0)
     unit(1)
@@ -332,11 +319,12 @@
     last(1, 1, -1)
     unit(6)
     close(4)
+    close(5)
     last(1, 1, 2)
     for oa in (-1, 1, 2):
         last(1, 0, oa)
     unit(7)
-    for g in (5, 6, 7):
+    for g in (6, 7):
         close(g)
 
     both = lax.broadcasted_iota(jnp.int32, (TS, 128), 1) % TS == lax.broadcasted_iota(jnp.int32, (TS, 128), 0)
@@ -373,7 +361,6 @@
         out_specs=pl.BlockSpec(memory_space=pl.ANY),
         scratch_shapes=[
             pltpu.VMEM((2, NX, UR, ROWS, K), bf),
-            pltpu.VMEM((2, RC, 32, K), bf),
             pltpu.VMEM((4, SH), jnp.int32),
             pltpu.VMEM((4, SH), jnp.int32),
             pltpu.SMEM((16,), f4),
@@ -392,7 +379,7 @@
             pltpu.VMEM((48, 16, 128), f4),
             pltpu.VMEM((16 * STEP, 128), f4),
             pltpu.VMEM((SH, TS, R), bf),
-            dma((NSEM,)), dma((NSEM,)), dma((4 * RC,)), dma((4 * RC,)), dma((2,)), dma((32,)), dma((16,)), dma((SH,)), dma((5,)),
+            dma((NSEM,)), dma((NSEM,)), dma((2 * RC,)), dma((2 * RC,)), dma((2,)), dma((32,)), dma((16,)), dma((SH,)), dma((5,)),
         ],
         compiler_params=pltpu.CompilerParams(collective_id=0, has_side_effects=True,
                                              vmem_limit_bytes=60 * 1024 * 1024),

time: 53.3 us -> 55.5 us (1.041); the launches traced: 53.2 us -> 54.7 us
  Pallas kernels: 51.4 us -> 52.9 us
    pallas_call x1, Pallas kernels: 51.4 us -> 52.9 us  [body(): pl.pallas_call(kernel, out_shape=jax.ShapeDtypeStruct((SH, TS, R), bf), i...]
where the time goes in v7:
time: 55.5 us; the launch traced here: 54.7 us
  Pallas kernels  52.9 us (95%)
  local copies, waits for them, and re-layouts  1.77 us (3%)
    pallas_call x1, Pallas kernels, body(): pl.pallas_call(kernel, out_shape=jax.ShapeDtypeStruct((SH, TS, R), bf), i...  52.9 us
    unnamed x1, local copies, waits for them, and re-layouts  1.77 us

profile of v7, /device:TPU:1, one launch (start us, length us, event | category | flops | bytes accessed | tf_op | source)
XLA Modules:
  0.0 54.7 jit_solution(15373956703762510139)
XLA Ops:
  0.0 52.9 %shard_map.55 = bf16[12,64,192]{2,1,0:T(8,128)(2,1)} custom-call(bf16[3,64,256]{2,1,0:T(8,128)(2,1)} %bitcast.5, bf16[12,32,256]{2,1,0:T(8,128)(2,1)} %shot_hbm.1, s32[4,12]{1,0:T(4,128)} %bitcast.6, s32[4,12]{1,0:T(4,128)} %bitcast.7, f32[16]{0:T(128)} %table_hbm.1), custom_call_target="tpu_custom_call" | custom-call | tf_op jit(solution)/shard_map/pallas_call | solution.py:357
  52.9 1.8 %copy.7 = bf16[64,12,192]{2,0,1:T(8,128)(2,1)} copy(bf16[64,12,192]{2,0,1:T(8,128)(2,1)} %bitcast.4) | data formatting | bytes 589824

commit v8 on v5

--- a/solution.py
+++ b/solution.py
@@ -171,15 +171,6 @@
     base(0, 0)
     base(0, 1)
 
-    for l in range(2):
-        xg[l, :, :, 0:HEAD, :] = jnp.zeros((NX, UR, HEAD, K), jnp.bfloat16)
-        xg[l, :, :, HEAD + TS:ROWS, :] = jnp.zeros((NX, UR, ROWS - HEAD - TS, K), jnp.bfloat16)
-    half_f32[...] = jnp.zeros_like(half_f32)
-
-    @pl.when(t == 0)
-    def _():
-        halo_in[...] = jnp.zeros_like(halo_in)
-
     for copy in small:
         copy.wait()
     wt[...] = jnp.zeros_like(wt)
@@ -201,6 +192,15 @@
     op_copy = start(remote(op_own, op_sib, op_sem.at[0], op_sem.at[1], sibling))
 
     round1(0)
+    for l in range(2):
+        xg[l, :, :, 0:HEAD, :] = jnp.zeros((NX, UR, HEAD, K), jnp.bfloat16)
+        xg[l, :, :, HEAD + TS:ROWS, :] = jnp.zeros((NX, UR, ROWS - HEAD - TS, K), jnp.bfloat16)
+    half_f32[...] = jnp.zeros_like(half_f32)
+
+    @pl.when(t == 0)
+    def _():
+        halo_in[...] = jnp.zeros_like(halo_in)
+
     z_second = []
     for i in range(RC):
         for d, who in ((0, up), (1, down)):

time: 53.3 us -> 53.3 us (level)
  no operation moved by 1% of the time
where the time goes in v8:
time: 53.3 us; the launch traced here: 53.2 us
  Pallas kernels  51.4 us (96%)
  local copies, waits for them, and re-layouts  1.77 us (3%)
    pallas_call x1, Pallas kernels, body(): pl.pallas_call(kernel, out_shape=jax.ShapeDtypeStruct((SH, TS, R), bf), i...  51.4 us
    unnamed x1, local copies, waits for them, and re-layouts  1.77 us

profile of v8, /device:TPU:1, one launch (start us, length us, event | category | flops | bytes accessed | tf_op | source)
XLA Modules:
  0.0 53.2 jit_solution(10397269498347681809)
XLA Ops:
  0.0 51.4 %shard_map.55 = bf16[12,64,192]{2,1,0:T(8,128)(2,1)} custom-call(bf16[3,64,256]{2,1,0:T(8,128)(2,1)} %bitcast.5, bf16[12,32,256]{2,1,0:T(8,128)(2,1)} %shot_hbm.1, s32[4,12]{1,0:T(4,128)} %bitcast.6, s32[4,12]{1,0:T(4,128)} %bitcast.7, f32[16]{0:T(128)} %table_hbm.1), custom_call_target="tpu_custom_call" | custom-call | tf_op jit(solution)/shard_map/pallas_call | solution.py:369
  51.4 1.8 %copy.7 = bf16[64,12,192]{2,0,1:T(8,128)(2,1)} copy(bf16[64,12,192]{2,0,1:T(8,128)(2,1)} %bitcast.4) | data formatting | bytes 589824

commit v9 on v8

--- a/solution.py
+++ b/solution.py
@@ -201,14 +201,6 @@
     def _():
         halo_in[...] = jnp.zeros_like(halo_in)
 
-    z_second = []
-    for i in range(RC):
-        for d, who in ((0, up), (1, down)):
-            z_first[i][d].wait_recv()
-            dst = xg.at[1, 0, pl.ds(i, 1), pl.ds(HEAD + HALF[d][0], 32)]
-            k = 2 * (RC + i) + d
-            z_second.append(start(remote(rz.at[d, pl.ds(i, 1)], dst, z_send.at[k], z_recv.at[k], who)))
-
     def place(ref, s, row):
         v = ref[s].astype(jnp.float32)
         for q in range(2):
@@ -223,6 +215,14 @@
         for a in range(2):
             cols = a * K + q * 128
             op_all[:, cols:cols + 128] = op_f32[q, a * LAG * SH:(a + 1) * LAG * SH, :].astype(jnp.bfloat16)
+
+    z_second = []
+    for i in range(RC):
+        for d, who in ((0, up), (1, down)):
+            z_first[i][d].wait_recv()
+            dst = xg.at[1, 0, pl.ds(i, 1), pl.ds(HEAD + HALF[d][0], 32)]
+            k = 2 * (RC + i) + d
+            z_second.append(start(remote(rz.at[d, pl.ds(i, 1)], dst, z_send.at[k], z_recv.at[k], who)))
 
     lane = lax.broadcasted_iota(jnp.int32, (S2, 128), 1)
 

time: 53.3 us -> 53.4 us (level)
  no operation moved by 1% of the time
where the time goes in v9:
time: 53.4 us; the launch traced here: 53.2 us
  Pallas kernels  51.4 us (96%)
  local copies, waits for them, and re-layouts  1.77 us (3%)
    pallas_call x1, Pallas kernels, body(): pl.pallas_call(kernel, out_shape=jax.ShapeDtypeStruct((SH, TS, R), bf), i...  51.4 us
    unnamed x1, local copies, waits for them, and re-layouts  1.77 us

profile of v9, /device:TPU:1, one launch (start us, length us, event | category | flops | bytes accessed | tf_op | source)
XLA Modules:
  0.0 53.2 jit_solution(4798167202726831172)
XLA Ops:
  0.0 51.4 %shard_map.55 = bf16[12,64,192]{2,1,0:T(8,128)(2,1)} custom-call(bf16[3,64,256]{2,1,0:T(8,128)(2,1)} %bitcast.5, bf16[12,32,256]{2,1,0:T(8,128)(2,1)} %shot_hbm.1, s32[4,12]{1,0:T(4,128)} %bitcast.6, s32[4,12]{1,0:T(4,128)} %bitcast.7, f32[16]{0:T(128)} %table_hbm.1), custom_call_target="tpu_custom_call" | custom-call | tf_op jit(solution)/shard_map/pallas_call | solution.py:369
  51.4 1.8 %copy.7 = bf16[64,12,192]{2,0,1:T(8,128)(2,1)} copy(bf16[64,12,192]{2,0,1:T(8,128)(2,1)} %bitcast.4) | data formatting | bytes 589824
